TPU v7x, 512 devices: a whole 4x4x16 slice. The times are simulated.
512 devices in a mesh: dp: 64 (over z, x), tensor: 8 (over y, core).
Axes of the slice: x: 4, y: 4, z: 16, core: 2. Of those that a mesh axis runs over, the one named last changes fastest.
Arguments:
- tokens: bfloat16 [8192, 5120], P('dp'), may hold values from -6 to 6
- w_value: bfloat16 [5120, 1024], P(None, 'tensor'), may hold values from -0.078125 to 0.078125
- b_value: bfloat16 [1024], P('tensor'), may hold values from -3 to 3
- d_values: bfloat16 [8192, 1024], P('dp', 'tensor'), may hold values from -1.1953125 to 1.1953125
- error_in: bfloat16 [327680, 1024], P('dp', 'tensor'), may hold values from -9 to 9
- q_init: float32 [1024, 32], P('tensor'), may hold values from -6 to 6
Outputs:
- values: bfloat16 [8192, 1024], P('dp', 'tensor')
- d_tokens: bfloat16 [8192, 5120], P(('dp', 'tensor'))
- error_out: bfloat16 [327680, 1024], P('dp', 'tensor')
- q_next: float32 [1024, 32], P('tensor')
- d_bias: float32 [1024], P('tensor')
All inputs are finite; a program needn't handle non-finite values.
Results may differ from a plain program's by a relative error of at most 0.017.
Values may be sent and summed in bfloat16 or wider, within the bound.
A program may use at most 64 MiB of HBM per device.

v0:
```python
import jax
import jax.numpy as jnp
from jax import lax
from jax.sharding import PartitionSpec as P


def factor_rows(rows, lower):
    return jax.scipy.linalg.solve_triangular(lower, rows.T, lower=True).T


def per_device(tokens, w_value, b_value, d_values, error_in, q_init):
    highest = lax.Precision.HIGHEST
    replicas = lax.axis_size("dp")
    values = (
        jnp.dot(tokens, w_value, preferred_element_type=jnp.float32) + b_value.astype(jnp.float32)
    ).astype(jnp.bfloat16)
    d_tokens = lax.psum_scatter(
        lax.dot_general(
            d_values, w_value, (((1,), (1,)), ((), ())), preferred_element_type=jnp.float32
        ).astype(jnp.bfloat16),
        "tensor",
        scatter_dimension=0,
        tiled=True,
    )
    bias_local = jnp.sum(d_values.astype(jnp.float32), axis=0)
    bias_total = lax.psum(bias_local, "dp")
    weight_grad = lax.dot_general(
        tokens, d_values, (((0,), (0,)), ((), ())), preferred_element_type=jnp.float32
    )
    merged = weight_grad + error_in.astype(jnp.float32)
    local_basis = jnp.dot(merged, q_init, precision=highest)
    basis = lax.psum(local_basis, "dp")
    gram = jnp.dot(basis.T, basis, precision=highest)
    basis_hat = factor_rows(basis, jnp.linalg.cholesky(gram))
    factor_local = jnp.dot(merged.T, basis_hat, precision=highest)
    factor_total = lax.psum(factor_local, "dp")
    q_next = factor_total / replicas
    approx = jnp.dot(basis_hat, q_next.T, precision=highest)
    error_out = (merged - approx).astype(jnp.bfloat16)
    d_bias = bias_total / replicas
    return (values, d_tokens, error_out, q_next, d_bias)


def solution(mesh):
    placed = (
        P("dp", None),
        P(None, "tensor"),
        P("tensor"),
        P("dp", "tensor"),
        P("dp", "tensor"),
        P("tensor", None),
    )
    return jax.shard_map(
        per_device,
        mesh=mesh,
        in_specs=placed,
        out_specs=(
            P("dp", "tensor"),
            P(("dp", "tensor"), None),
            P("dp", "tensor"),
            P("tensor", None),
            P("tensor"),
        ),
        check_vma=False,
    )
```

profile of v0, /device:TPU:8, one launch (start us, length us, event | category | flops | bytes accessed | tf_op | source)
XLA Modules:
  0.0 590.9 jit_solution(13364633290394591193)
XLA Ops:
  8.0 0.0 copy-start
  8.0 0.0 copy-start.6
  8.0 0.0 all-reduce.3.cloned.1.call-start
  8.1 1.3 copy-done
  9.3 1.9 convolution_add_fusion
  11.2 0.0 copy-start.1
  11.2 1.5 copy-done.1
  12.7 0.0 copy-done.6
  12.7 0.0 copy-start.3
  12.7 0.0 copy-start.4
  12.7 3.5 fusion.6
  16.3 0.0 all-reduce.3.cloned.1.call-update
  16.3 0.0 reduce-scatter.2.cloned.1.call-start
  16.3 0.0 copy-done.3
  16.4 0.0 copy-done.4
  16.4 1.6 convolution_convert_fusion
  18.0 0.0 copy-start.7
  18.0 0.0 reduce-scatter.2.cloned.1.call-update
  18.0 0.6 copy-done.7
  18.6 1.1 fusion.1
  19.7 267.0 %all-reduce.3.cloned.1.call-done = f32[5120,32]{0,1:T(8,128)} async-done(((f32[5120,32]{0,1:T(8,128)}), f32[5120,32]{0,1:T(8,128)}) %all-reduce.3.cloned.1.call-update) | async-done | bytes 655376 | tf_op jit(solution)/shard_map/psum | solution.py:32
  286.8 0.0 copy-start.2
  286.8 2.0 fusion.7
  288.8 0.1 copy.11
  288.9 2.9 cholesky.16
  291.8 0.6 compare_reduce_fusion
  292.5 0.7 fusion.2
  293.1 2.4 custom-call.7
  295.5 0.0 copy-done.2
  295.5 0.8 fusion.3
  296.3 3.3 fusion.8
  299.6 276.7 %all-reduce = (f32[128,32]{0,1:T(8,128)S(1)}, f32[128]{0:T(128)S(1)}) all-reduce(f32[128,32]{0,1:T(8,128)S(1)} %fusion.8, f32[128]{0:T(128)S(1)} %convert_reduce_fusion), channel_id=1, replica_groups=mesh['dp'=64,'tensor'=8] {'dp'}, use_global_device_ids=true, to_apply=%region_4.5 | all-reduce | flops 4224 | bytes 33792 | tf_op jit(solution)/shard_map/psum | solution.py:36
  576.3 0.5 broadcast_multiply_fusion.1
  576.8 0.0 copy-start.5
  576.8 6.6 %fusion = bf16[5120,128]{1,0:T(8,128)(2,1)} fusion(f32[5120,128]{1,0:T(8,128)} %copy-done.1, f32[32,5120]{1,0:T(8,128)S(1)} %fusion.3, f32[128,32]{0,1:T(8,128)S(1)} %broadcast_multiply_fusion), kind=kOutput, calls=%fused_computation.2 | convolution fusion | flops 252968960 | bytes 4603904 | tf_op jit(solution)/shard_map/dot_general | solution.py:38
  583.5 0.0 copy-done.5
  583.5 0.0 reduce-scatter.2.cloned.1.call-done
  (5 shorter events, 0.1 us)
Async XLA Ops:
  8.0 1.3 copy-start
  8.0 4.7 copy-start.6
  8.0 278.7 %all-reduce.3.cloned.1.call-start = ((), (), s32[]{:S(2)}) async-start(), calls=%async_computation.2 | async-start | bytes 1310720 | tf_op jit(solution)/shard_map/psum | solution.py:32
  11.2 1.5 copy-start.1
  12.7 3.6 copy-start.3
  12.7 3.6 copy-start.4
  16.3 567.2 %reduce-scatter.2.cloned.1.call-start = ((), (), s32[]{:S(2)}) async-start(), calls=%async_computation.1 | async-start | bytes 1474560 | tf_op jit(solution)/shard_map/reduce_scatter | solution.py:17
  18.0 0.7 copy-start.7
  286.8 8.8 %copy-start.2 = (f32[5120,32]{0,1:T(8,128)S(1)}, f32[5120,32]{0,1:T(8,128)}, u32[]{:S(2)}) copy-start(f32[5120,32]{0,1:T(8,128)} %all-reduce.3.cloned.1.call-done) | copy-start | bytes 1966084
  576.8 6.6 %copy-start.5 = (f32[128,32]{0,1:T(8,128)}, f32[128,32]{0,1:T(8,128)S(1)}, u32[]{:S(2)}) copy-start(f32[128,32]{0,1:T(8,128)S(1)} %broadcast_multiply_fusion) | copy-start | bytes 49156
Sparse Core Ops, SparseCore 0:
  16.4 270.2 all-reduce.2
Sparse Core Ops, SparseCore 1:
  20.2 41.5 reduce-scatter.1
where the time goes:
time: 591 us
  blocking collectives  277 us (47%)
  waiting for transfers between devices  267 us (45%)
  matrix products  20.8 us (4%)
  between operations  15.6 us (3%)
  other arithmetic  7.24 us (1%)
    psum x1, blocking collectives, per_device(): factor_total = lax.psum(factor_local, 'dp')  277 us
    psum x1, waiting for transfers between devices, per_device(): basis = lax.psum(local_basis, 'dp')  267 us
  transfers between devices with their start and end apart: 2, of which 1 were waited for; matrix products, arithmetic and copies ran while one was open for 4% of the time, Pallas kernels for 0%

commit v1 on v0

v1 whole, which is shorter than its diff:
```python
import functools

import jax
import jax.numpy as jnp
from jax import lax
from jax.experimental import pallas as pl
from jax.experimental.pallas import tpu as pltpu
from jax.sharding import PartitionSpec as P

MESH = pl.DeviceIdType.MESH
F32 = jnp.float32
BF16 = jnp.bfloat16
NX = 4
NQ = 4
NN = ((1,), (0,))
NT = ((1,), (1,))
TN = ((0,), (0,))


def dot(a, b, dims, precision=None):
    return lax.dot_general(a, b, (dims, ((), ())), preferred_element_type=F32, precision=precision)


def split(v):
    high = v.astype(BF16)
    low = (v - high.astype(F32)).astype(BF16)
    return jnp.concatenate([high, low], axis=0)


def fold(v):
    n = v.shape[0] // 2
    return v[:n] + v[n:]


def inverse_lower(gram):
    n = gram.shape[0]
    row = lax.broadcasted_iota(jnp.int32, (n, n), 0)
    col = lax.broadcasted_iota(jnp.int32, (n, n), 1)
    a = gram
    inv = (row == col).astype(F32)
    for k in range(0, n, 2):
        col0, col1 = a[:, k : k + 1], a[:, k + 1 : k + 2]
        above = a[k : k + 1, k + 1 : k + 2]
        scale0 = 1.0 / a[k : k + 1, k : k + 1]
        step = a[k + 1 : k + 2, k : k + 1] * scale0
        scale1 = 1.0 / (a[k + 1 : k + 2, k + 1 : k + 2] - step * above)
        factor0 = jnp.where(row[:, :1] > k, col0 * scale0, 0.0)
        factor1 = jnp.where(row[:, :1] > k + 1, (col1 - factor0 * above) * scale1, 0.0)

        def eliminate(v):
            row0, row1 = v[k : k + 1, :], v[k + 1 : k + 2, :]
            return v - factor0 * row0 - factor1 * (row1 - step * row0)

        a, inv = eliminate(a), eliminate(inv)
    pivots = jnp.sum(jnp.where(row == col, a, 0.0), axis=1, keepdims=True)
    return inv / jnp.sqrt(pivots)


def kernel(
    nz, ny,
    tok_h, w_h, b_h, dv_h, e_h, q_h,
    vo, dto, m, bt, back, qno, dbo,
    xv, wv, ev, dvv, qv, bv,
    bxs, bxr, own, zs, zr, bf, ms, rl, mr, mx, gs,
    tsx, trx, tz, tf, bx, bz,
    pr, po, ys, yr,
    in_sem,
    ms_s, rl_r, mr_r, gss_s, gsr_s,
    bxs_s, bxr_s, zs_s, zr_s, ags_s, agr_s, axs_s, axr_s,
    tsx_s, trx_s, tzs_s, tzr_s, tfs_s, tfr_s,
    bias_xs, bias_xr, bias_zs, bias_zr, ps_s, pr_s, ys_s, yr_s,
):
    d_model = wv.shape[0]
    dq = d_model // NX
    dh = dq // 2
    zg = nz // NQ
    replicas = nz * NX
    dp, t = lax.axis_index("dp"), lax.axis_index("tensor")
    z, x = dp // NX, dp % NX
    y, c = t // 2, t % 2
    sib = t + 1 - 2 * c

    def at_x(xx):
        return (z * NX + xx, t)

    def at_z(zz):
        return (zz * NX + x, t)

    def at_y(yy):
        return (dp, yy * 2 + c)

    def nx(d):
        return (x + d) % NX

    def nzz(d):
        return (z + d) % nz

    def nyy(d):
        return (y + d) % ny

    x_order = (2, 1, 3)
    y_order = tuple(sorted(range(1, ny), key=lambda d: -min(d, ny - d)))
    z_order = tuple(sorted(range(1, nz), key=lambda d: -min(d, nz - d)))

    loads = {}
    for i, (name, src, dst) in enumerate(
        (("dv", dv_h, dvv), ("q", q_h, qv), ("e", e_h, ev), ("x", tok_h, xv), ("w", w_h, wv), ("b", b_h, bv))
    ):
        loads[name] = pltpu.make_async_copy(src, dst, in_sem.at[i])
        loads[name].start()

    barrier = pltpu.get_barrier_semaphore()
    peers = [at_x(nx(d)) for d in x_order] + [at_z(nzz(d)) for d in z_order]
    peers += [at_y(nyy(d)) for d in y_order] + [(dp, sib)]
    for peer in peers:
        pl.semaphore_signal(barrier, inc=1, device_id=peer, device_id_type=MESH)

    def remote(src, dst, send, recv, peer):
        return pltpu.make_async_remote_copy(
            src_ref=src, dst_ref=dst, send_sem=send, recv_sem=recv, device_id=peer, device_id_type=MESH
        )

    def arrived(ref, sem, peer):
        remote(ref, ref, sem, sem, peer).wait_recv()

    sent = []

    def send(*args):
        copy = remote(*args)
        copy.start()
        sent.append(copy)

    def columns(j):
        return pl.ds(pl.multiple_of(j * dq, 128), dq)

    loads["dv"].wait()
    loads["q"].wait()
    q_pair = split(qv[...])
    mixed = fold(dot(q_pair, dvv[...], NT))
    mixed_pair = split(mixed)
    loads["e"].wait()
    loads["x"].wait()

    def local_basis(j, half):
        cols = pl.ds(pl.multiple_of(j * dq + half * dh, 128), dh)
        return fold(dot(q_pair, ev[cols, :], NT) + dot(mixed_pair, xv[:, cols], NN))

    for half in range(2):
        for d in x_order:
            bxs[d, half] = local_basis(nx(d), half).astype(BF16)
    pl.semaphore_wait(barrier, len(peers))
    for half in range(2):
        for d in x_order:
            send(
                bxs.at[d, half], bxr.at[x, half], bxs_s.at[d, half], bxr_s.at[x, half], at_x(nx(d))
            )
    for half in range(2):
        own[half] = local_basis(x, half)

    def merged(j):
        cols = columns(j)
        m[cols, :] = dot(xv[:, cols], dvv[...], TN) + ev[cols, :].astype(F32)
        return m[cols, :]

    far = merged(nx(2)).astype(BF16)
    for h, d in ((0, 1), (1, 3)):
        ms[2, h] = far[h * dh : (h + 1) * dh]
        send(ms.at[2, h], rl.at[h], ms_s.at[2, h], rl_r.at[h], at_x(nx(d)))

    owner_pos = (zg - 1) // 2 + c
    mine = z // zg
    is_owner = z % zg == owner_pos

    def to_owner(qq):
        tgt = qq * zg + owner_pos
        return tgt, remote(zs.at[qq], zr.at[z], zs_s.at[qq], zr_s.at[z], at_z(tgt))

    for half in range(2):
        total = own[half]
        for d in x_order[::-1]:
            arrived(bxr.at[nx(d), half], bxr_s.at[nx(d), half], at_x(nx(d)))
            total = total + bxr[nx(d), half].astype(F32)
        for g in range(2):
            qq = 2 * g + half
            zs[qq] = total[16 * g : 16 * g + 16].astype(BF16)
            tgt, copy = to_owner(qq)
            pl.when(z != tgt)(copy.start)

    for h, d in ((0, 1), (1, 3)):
        near = merged(nx(d)).astype(BF16)
        ms[d, 1 - h] = near[(1 - h) * dh : (2 - h) * dh]
        send(ms.at[d, 1 - h], mr.at[h, 1 - h], ms_s.at[d, 1 - h], mr_r.at[h, 1 - h], at_x(nx(d)))

    loads["w"].wait()
    for k in range(NX):
        cols = slice(k * dq, (k + 1) * dq)
        p = dot(dvv[...], wv[cols, :], NT).astype(BF16)
        for yy in range(ny):
            for cc in range(2):
                first = (2 * yy + cc) * 16
                po[yy, cc, :, cols] = p[first : first + 16]
    for yy in range(ny):
        send(po.at[yy, 1 - c], pr.at[yy], ps_s.at[yy], pr_s.at[yy], (dp, sib))
    merged(x)
    for h, d in ((0, 1), (1, 3)):
        arrived(rl.at[h], rl_r.at[h], at_x(nx(4 - d)))
        rows = pl.ds(pl.multiple_of(nx(d) * dq + h * dh, 128), dh)
        ms[d, h] = (m[rows, :] + rl[h].astype(F32)).astype(BF16)
        send(ms.at[d, h], mr.at[h, h], ms_s.at[d, h], mr_r.at[h, h], at_x(nx(d)))

    def block(qq):
        g, half = qq // 2, qq % 2
        return bf.at[x, pl.ds(pl.multiple_of(g * 16, 16), 16), pl.ds(pl.multiple_of(half * dh, 128), dh)]

    def from_owner(d):
        return remote(block(mine), block(mine), ags_s.at[d], agr_s.at[mine], at_z(nzz(d)))

    @pl.when(is_owner)
    def _():
        acc = zs[mine].astype(F32)
        for d in z_order[::-1]:
            arrived(zr.at[nzz(d)], zr_s.at[nzz(d)], at_z(nzz(d)))
            acc = acc + zr[nzz(d)].astype(F32)
        block(mine)[...] = acc.astype(BF16)
        for d in z_order:
            from_owner(d).start()

    bx[x] = jnp.sum(dvv[...].astype(F32), axis=0, keepdims=True)
    for d in x_order:
        send(bx.at[x], bx.at[x], bias_xs.at[d], bias_xr.at[x], at_x(nx(d)))

    loads["b"].wait()
    vo[...] = (dot(xv[...], wv[...], NN) + bv[...].astype(F32)).astype(BF16)

    for d in y_order + (0,):
        yy = nyy(d)
        arrived(pr.at[yy], pr_s.at[yy], (dp, sib))
        ys[yy] = (po[yy, c].astype(F32) + pr[yy].astype(F32)).astype(BF16)
        if d:
            send(ys.at[yy], yr.at[y], ys_s.at[d], yr_s.at[y], at_y(yy))

    for h in range(2):
        total = m[pl.ds(pl.multiple_of(x * dq + h * dh, 128), dh), :]
        for slot, d in ((0, 3), (1, 1)):
            arrived(mr.at[slot, h], mr_r.at[slot, h], at_x(nx(d)))
            total = total + mr[slot, h].astype(F32)
        mx[2 * h * dh : 2 * (h + 1) * dh, :] = split(total)

    for qq in range(NQ):
        tgt = qq * zg + owner_pos

        @pl.when(z != tgt)
        def _():
            arrived(block(qq), agr_s.at[qq], at_z(tgt))

    basis = bf[x]
    factor = sum(
        dot(basis[:, h * dh : (h + 1) * dh], mx[k * dh : (k + 1) * dh, :], NN) for k in range(4) for h in (k // 2,)
    )
    for j in range(NX):
        tsx[j] = factor[8 * j : 8 * j + 8]
    for d in x_order:
        send(tsx.at[nx(d)], trx.at[x], tsx_s.at[d], trx_s.at[x], at_x(nx(d)))
    trx[x] = tsx[x]
    gs[x] = dot(basis, basis, NT)
    for d in x_order:
        send(gs.at[x], gs.at[x], gss_s.at[d], gsr_s.at[x], at_x(nx(d)))
    for d in x_order:
        send(bf.at[x], bf.at[x], axs_s.at[d], axr_s.at[x], at_x(nx(d)))

    for d in x_order[::-1]:
        arrived(trx.at[nx(d)], trx_s.at[nx(d)], at_x(nx(d)))
    tz[z] = (trx[0] + trx[1]) + (trx[2] + trx[3])
    for d in z_order:
        send(tz.at[z], tz.at[z], tzs_s.at[d], tzr_s.at[z], at_z(nzz(d)))

    for d in x_order:
        arrived(bx.at[nx(d)], bias_xr.at[nx(d)], at_x(nx(d)))
    bz[z] = (bx[0] + bx[1]) + (bx[2] + bx[3])
    for d in z_order:
        send(bz.at[z], bz.at[z], bias_zs.at[d], bias_zr.at[z], at_z(nzz(d)))

    for d in x_order[::-1]:
        arrived(gs.at[nx(d)], gsr_s.at[nx(d)], at_x(nx(d)))
    gram = (gs[0] + gs[1]) + (gs[2] + gs[3])
    inv = inverse_lower(gram)
    project = jnp.concatenate([inv, dot(inv, inv, TN, lax.Precision.HIGHEST)], axis=0) / replicas

    def by_rows(j):
        b = bf[j]
        bt[columns(j), :] = jnp.concatenate([b, b], axis=0).T

    by_rows(x)
    for d in z_order[::-1]:
        arrived(tz.at[nzz(d)], tzr_s.at[nzz(d)], at_z(nzz(d)))
    total = tz[0]
    for s in range(1, nz):
        total = total + tz[s]
    tf[x] = total
    for d in x_order:
        send(tf.at[x], tf.at[x], tfs_s.at[d], tfr_s.at[x], at_x(nx(d)))

    for d in x_order[::-1]:
        arrived(bf.at[nx(d)], axr_s.at[nx(d)], at_x(nx(d)))
        by_rows(nx(d))
    acc = ys[y].astype(F32)
    for d in y_order[::-1]:
        arrived(yr.at[nyy(d)], yr_s.at[nyy(d)], at_y(nyy(d)))
        acc = acc + yr[nyy(d)].astype(F32)
    dto[...] = acc.astype(BF16)
    for d in z_order[::-1]:
        arrived(bz.at[nzz(d)], bias_zr.at[nzz(d)], at_z(nzz(d)))
    total = bz[0]
    for s in range(1, nz):
        total = total + bz[s]
    dbo[...] = total / replicas

    for d in x_order[::-1]:
        arrived(tf.at[nx(d)], tfr_s.at[nx(d)], at_x(nx(d)))
    factor = tf[...].reshape(NX * 8, 128)
    both = dot(project, factor, NN, lax.Precision.HIGHEST)
    back[...] = split(both[NX * 8 :])
    qno[...] = both[: NX * 8]

    for qq in range(NQ):
        tgt, copy = to_owner(qq)
        pl.when(z != tgt)(copy.wait_send)

    @pl.when(is_owner)
    def _():
        for d in z_order:
            from_owner(d).wait_send()

    for copy in sent:
        copy.wait_send()


def finish(vo, dto, m, bt, back, qno, dbo, val_h, dt_h, err_h, qn_h, db_h, eo, sem):
    copies = []

    def store(src, dst):
        copy = pltpu.make_async_copy(src, dst, sem.at[len(copies)])
        copy.start()
        copies.append(copy)

    for src, dst in ((dto, dt_h), (vo, val_h), (qno, qn_h), (dbo, db_h)):
        store(src, dst)
    dq = m.shape[0] // NX
    for k in range(NX):
        rows = slice(k * dq, (k + 1) * dq)
        eo[rows, :] = (m[rows, :] - dot(bt[rows, :], back[...], NN)).astype(BF16)
        store(eo.at[pl.ds(k * dq, dq), :], err_h.at[pl.ds(k * dq, dq), :])
    for copy in copies:
        copy.wait()


def per_device(nz, ny, tokens, w_value, b_value, d_values, error_in, q_init):
    rows, d_model = tokens.shape
    head, rank = q_init.shape
    dq = d_model // NX
    dh = dq // 2
    dma = pltpu.SemaphoreType.DMA
    any_spec = pl.BlockSpec(memory_space=pl.ANY)
    hbm = pl.BlockSpec(memory_space=pltpu.HBM)
    vmem = pltpu.VMEM
    scratch = [
        vmem((rows, d_model), BF16), vmem((d_model, head), BF16), vmem((d_model, head), BF16),
        vmem((rows, head), BF16), vmem((rank, head), F32), vmem((1, head), BF16),
        vmem((NX, 2, rank, dh), BF16), vmem((NX, 2, rank, dh), BF16), vmem((2, rank, dh), F32),
        vmem((NQ, 16, dh), BF16), vmem((nz, 16, dh), BF16), vmem((NX, rank, dq), BF16),
        vmem((NX, 2, dh, head), BF16), vmem((2, dh, head), BF16), vmem((2, 2, dh, head), BF16),
        vmem((2 * dq, head), BF16),
        vmem((NX, rank, rank), F32),
        vmem((NX, 8, head), F32), vmem((NX, 8, head), F32), vmem((nz, 8, head), F32), vmem((NX, 8, head), F32),
        vmem((NX, 1, head), F32), vmem((nz, 1, head), F32),
    ]
    scratch += [vmem((ny, 16, d_model), BF16), vmem((ny, 2, 16, d_model), BF16)]
    scratch += [vmem((ny, 16, d_model), BF16)] * 2
    scratch += [
        dma((6,)),
        dma((NX, 2)), dma((2,)), dma((2, 2)), dma((NX,)), dma((NX,)),
        dma((NX, 2)), dma((NX, 2)), dma((NQ,)), dma((nz,)), dma((nz,)), dma((NQ,)), dma((NX,)), dma((NX,)),
        dma((NX,)), dma((NX,)), dma((nz,)), dma((nz,)), dma((NX,)), dma((NX,)),
        dma((NX,)), dma((NX,)), dma((nz,)), dma((nz,)), dma((ny,)), dma((ny,)), dma((ny,)), dma((ny,)),
    ]
    held = pl.BlockSpec(memory_space=pltpu.VMEM)
    operands = (tokens, w_value, b_value.reshape(1, head), d_values, error_in, q_init.T)
    parts = pl.pallas_call(
        functools.partial(kernel, nz, ny),
        out_shape=(
            vmem((rows, head), BF16),
            vmem((16, d_model), BF16),
            vmem((d_model, head), F32),
            vmem((d_model, 2 * rank), BF16),
            vmem((2 * rank, head), BF16),
            vmem((rank, head), F32),
            vmem((1, head), F32),
        ),
        in_specs=[hbm] * 6,
        out_specs=(held,) * 7,
        scratch_shapes=scratch,
        compiler_params=pltpu.CompilerParams(
            collective_id=0, has_side_effects=True, vmem_limit_bytes=48 * 1024 * 1024
        ),
        name="reduce_factors",
    )(*[pltpu.with_memory_space_constraint(a, pltpu.HBM) for a in operands])
    values, d_tokens, error_out, q_next, d_bias = pl.pallas_call(
        finish,
        out_shape=(
            jax.ShapeDtypeStruct((rows, head), BF16),
            jax.ShapeDtypeStruct((16, d_model), BF16),
            jax.ShapeDtypeStruct((d_model, head), BF16),
            jax.ShapeDtypeStruct((rank, head), F32),
            jax.ShapeDtypeStruct((1, head), F32),
        ),
        in_specs=[held] * 7,
        out_specs=(any_spec,) * 5,
        scratch_shapes=[vmem((d_model, head), BF16), dma((8,))],
        compiler_params=pltpu.CompilerParams(vmem_limit_bytes=16 * 1024 * 1024),
        name="store_results",
    )(*parts)
    return values, d_tokens, error_out, q_next.T, d_bias.reshape(head)


def solution(mesh):
    nz = mesh.shape["dp"] // NX
    ny = mesh.shape["tensor"] // 2
    placed = (
        P("dp", None),
        P(None, "tensor"),
        P("tensor"),
        P("dp", "tensor"),
        P("dp", "tensor"),
        P("tensor", None),
    )
    return jax.shard_map(
        functools.partial(per_device, nz, ny),
        mesh=mesh,
        in_specs=placed,
        out_specs=(
            P("dp", "tensor"),
            P(("dp", "tensor"), None),
            P("dp", "tensor"),
            P("tensor", None),
            P("tensor"),
        ),
        check_vma=False,
    )
```

time: 591 us -> 53.6 us (0.09)
  blocking collectives: 277 us -> 0 us
  waiting for transfers between devices: 267 us -> 0 us
  Pallas kernels: 0 us -> 52.8 us
  matrix products: 20.8 us -> 0 us
  between operations: 15.6 us -> 0.64 us
  other arithmetic: 7.24 us -> 0 us
    psum x1 -> x0, blocking collectives: 277 us -> none  [per_device(): factor_total = lax.psum(factor_local, 'dp')]
    psum x1 -> x0, waiting for transfers between devices: 267 us -> none  [per_device(): basis = lax.psum(local_basis, 'dp')]
    pallas_call x0 -> x2, Pallas kernels: none -> 52.8 us  [the longest x1 51.4 us: per_device(): pl.pallas_call(functools.partial(kernel, nz, ny), out_shape=(vmem((rows,...]
    dot_general x7 -> x0, matrix products: 20.1 us -> none  [the longest x1 6.62 us: per_device(): approx = jnp.dot(basis_hat, q_next.T, precision=highest)]
    another operation x5 -> x0, other arithmetic: 6.68 us -> none  [the longest x3 3.6 us: per_device(): basis_hat = factor_rows(basis, jnp.linalg.cholesky(gram))]
  transfers between devices with their start and end apart: 2 -> 0, of which waited for: 1 -> 0; matrix products, arithmetic and copies ran while one was open for 4% -> 0% of each run, Pallas kernels for 0% -> 0%
where the time goes in v1:
time: 53.6 us; the launch traced here: 53.5 us
  Pallas kernels  52.8 us (99%)
  between operations  0.64 us (1%)
    pallas_call x1, Pallas kernels, per_device(): pl.pallas_call(functools.partial(kernel, nz, ny), out_shape=(vmem((rows,...  51.4 us
    pallas_call x1, Pallas kernels, per_device(): pl.pallas_call(finish, out_shape=(jax.ShapeDtypeStruct((rows, head), BF16...  1.43 us

profile of v1, /device:TPU:8, one launch (start us, length us, event | category | flops | bytes accessed | tf_op | source)
XLA Modules:
  0.0 53.5 jit_solution(12721753558718129875)
XLA Ops:
  0.6 51.4 %reduce_factors.1 = (bf16[128,128]{1,0:T(8,128)(2,1)S(1)}, bf16[16,5120]{1,0:T(8,128)(2,1)S(1)}, f32[5120,128]{1,0:T(8,128)S(1)}, bf16[5120,64]{1,0:T(8,128)(2,1...) custom-call(bf16[128,5120]{1,0:T(8,128)(2,1)} %tok_h.1, bf16[5120,128]{1,0:T(8,128)(2,1)} %w_h.1, ...), custom_call_target="tpu_custom_call" | custom-call | tf_op jit(solution)/shard_map/reduce_factors/pallas_call | solution.py:388
  52.0 1.4 %store_results.1 = (bf16[128,128]{1,0:T(8,128)(2,1)}, bf16[16,5120]{1,0:T(8,128)(2,1)}, bf16[5120,128]{1,0:T(8,128)(2,1)}, f32[32,128]{1,0:T(8,128)}, f32[1,128]{1,0:T(1,128)}) custom-call(bf16[128,128]{1,0:T(8,128)(2,1)S(1)} %get-tuple-element.17.vo, bf16[16,5120]{1,0:T(8,128)(2,1)S(1)} %get-tuple-element.18.dto, f32[5120,128]{1,0:T(8,128)S(1)} %get-tuple-element.19.m, ...), custom_call_target="tpu_custom_call" | custom-call | tf_op jit(solution)/shard_map/store_results/pallas_call | solution.py:407

commit v2 on v1

--- a/solution.py
+++ b/solution.py
@@ -191,6 +191,13 @@
         ms[d, 1 - h] = near[(1 - h) * dh : (2 - h) * dh]
         send(ms.at[d, 1 - h], mr.at[h, 1 - h], ms_s.at[d, 1 - h], mr_r.at[h, 1 - h], at_x(nx(d)))
 
+    merged(x)
+    for h, d in ((0, 1), (1, 3)):
+        arrived(rl.at[h], rl_r.at[h], at_x(nx(4 - d)))
+        rows = pl.ds(pl.multiple_of(nx(d) * dq + h * dh, 128), dh)
+        ms[d, h] = (m[rows, :] + rl[h].astype(F32)).astype(BF16)
+        send(ms.at[d, h], mr.at[h, h], ms_s.at[d, h], mr_r.at[h, h], at_x(nx(d)))
+
     loads["w"].wait()
     for k in range(NX):
         cols = slice(k * dq, (k + 1) * dq)
@@ -201,12 +208,6 @@
                 po[yy, cc, :, cols] = p[first : first + 16]
     for yy in range(ny):
         send(po.at[yy, 1 - c], pr.at[yy], ps_s.at[yy], pr_s.at[yy], (dp, sib))
-    merged(x)
-    for h, d in ((0, 1), (1, 3)):
-        arrived(rl.at[h], rl_r.at[h], at_x(nx(4 - d)))
-        rows = pl.ds(pl.multiple_of(nx(d) * dq + h * dh, 128), dh)
-        ms[d, h] = (m[rows, :] + rl[h].astype(F32)).astype(BF16)
-        send(ms.at[d, h], mr.at[h, h], ms_s.at[d, h], mr_r.at[h, h], at_x(nx(d)))
 
     def block(qq):
         g, half = qq // 2, qq % 2

time: 53.6 us -> 53.6 us (level)
  no operation moved by 1% of the time
where the time goes in v2:
time: 53.6 us; the launch traced here: 53.5 us
  Pallas kernels  52.8 us (99%)
  between operations  0.64 us (1%)
    pallas_call x1, Pallas kernels, per_device(): pl.pallas_call(functools.partial(kernel, nz, ny), out_shape=(vmem((rows,...  51.4 us
    pallas_call x1, Pallas kernels, per_device(): pl.pallas_call(finish, out_shape=(jax.ShapeDtypeStruct((rows, head), BF16...  1.43 us

profile of v2, /device:TPU:8, one launch (start us, length us, event | category | flops | bytes accessed | tf_op | source)
XLA Modules:
  0.0 53.5 jit_solution(1350253800981545140)
XLA Ops:
  0.6 51.4 %reduce_factors.1 = (bf16[128,128]{1,0:T(8,128)(2,1)S(1)}, bf16[16,5120]{1,0:T(8,128)(2,1)S(1)}, f32[5120,128]{1,0:T(8,128)S(1)}, bf16[5120,64]{1,0:T(8,128)(2,1...) custom-call(bf16[128,5120]{1,0:T(8,128)(2,1)} %tok_h.1, bf16[5120,128]{1,0:T(8,128)(2,1)} %w_h.1, ...), custom_call_target="tpu_custom_call" | custom-call | tf_op jit(solution)/shard_map/reduce_factors/pallas_call | solution.py:389
  52.0 1.4 %store_results.1 = (bf16[128,128]{1,0:T(8,128)(2,1)}, bf16[16,5120]{1,0:T(8,128)(2,1)}, bf16[5120,128]{1,0:T(8,128)(2,1)}, f32[32,128]{1,0:T(8,128)}, f32[1,128]{1,0:T(1,128)}) custom-call(bf16[128,128]{1,0:T(8,128)(2,1)S(1)} %get-tuple-element.17.vo, bf16[16,5120]{1,0:T(8,128)(2,1)S(1)} %get-tuple-element.18.dto, f32[5120,128]{1,0:T(8,128)S(1)} %get-tuple-element.19.m, ...), custom_call_target="tpu_custom_call" | custom-call | tf_op jit(solution)/shard_map/store_results/pallas_call | solution.py:408
